TPU v7x, 32 devices: a whole 2x2x4 slice. The times are simulated.
32 devices in a mesh: groups: 2 (over x), patch: 16 (over z, y, core).
Axes of the slice: x: 2, y: 2, z: 4, core: 2. Of those that a mesh axis runs over, the one named last changes fastest.
Arguments:
- template: float32 [64, 32768], P(None, ('groups', 'patch')), parts along dimension 1, may hold values from -6 to 6
- science: float32 [512, 4, 128], P(('groups', 'patch')), parts along dimension 0, may hold values from -6 to 6
- dest: int32 [512, 1], P(('groups', 'patch')), parts along dimension 0, may hold values from 0 to 15; in each aligned block of 16 rows (0 to 15, 16 to 31, ...) at most 2 rows name the same one
- row_offset: int32 [512], P(('groups', 'patch')), parts along dimension 0, may hold values from 0 to 60
- col_block: int32 [512], P(('groups', 'patch')), parts along dimension 0, may hold values from 0 to 7
- basis_rows: float32 [27, 21], replicated, may hold values from -1.25 to 1.25
- basis_cols: float32 [27, 21], replicated, may hold values from -1.25 to 1.25
- stamp_rows: int32 [32, 24], P('groups'), parts along dimension 0, may hold values from 0 to 63
- stamp_cols: int32 [32, 24], P('groups'), parts along dimension 0, may hold values from 0 to 1023
Outputs:
- difference: float32 [512, 4, 128], P(('groups', 'patch')), parts along dimension 0
There are 2 independent parts, one for each index of `groups`. A program takes and returns all parts, laid end to end along the dimension named above; an argument that names none is the same for every part. Nothing has to cross between parts.
Inputs may be any that keep to these rules, and one draw needn't show every extreme that they name: `dest`: each visit sends at most 2 strips to one sub-patch, and in every draw some visit sends exactly 2 to one.
All inputs are finite; a program needn't handle non-finite values.
Results may differ from a plain program's by a relative error of at most 0.0003.
Values sent between devices are 32-bit elements; how exact they have to be, the bound alone decides.
A program may use at most 64 MiB of HBM per device.

v0:
```python
import math

import jax
import jax.numpy as jnp
from jax import lax
from jax.sharding import PartitionSpec as P

CAP = 2
STAMP_HALF = 10


HIGH = lax.Precision.HIGHEST
RIDGE = 1.0


def with_halo(cells, sides, width):
    for axis, dim in sides:
        count = lax.axis_size(axis)
        ends = count - 1
        head = lax.slice_in_dim(cells, 0, width, axis=dim)
        tail = lax.slice_in_dim(cells, cells.shape[dim] - width, cells.shape[dim], axis=dim)
        cells = jnp.concatenate(
            [
                lax.ppermute(tail, axis, [(i, (i + 1) % count) for i in range(ends)]),
                cells,
                lax.ppermute(head, axis, [((i + 1) % count, i) for i in range(ends)]),
            ],
            axis=dim,
        )
    return cells


def filter_field(padded, row_taps, col_taps):
    taps = row_taps.shape[0]
    out_rows = padded.shape[0] - taps + 1
    out_cols = padded.shape[1] - taps + 1
    across = jnp.zeros((padded.shape[0], out_cols), jnp.float32)
    for shift_tap in range(taps):
        across = across + col_taps[shift_tap] * padded[:, shift_tap : shift_tap + out_cols]
    result = jnp.zeros((out_rows, out_cols), jnp.float32)
    for shift_tap in range(taps):
        result = result + row_taps[shift_tap] * across[shift_tap : shift_tap + out_rows, :]
    return result


def stamp_mask(row_start, blocks, stamp_r, stamp_c, strip_rows, block_cols):
    rows_here = row_start[:, None] + jnp.arange(strip_rows, dtype=jnp.int32)[None, :]
    cols_here = blocks[:, None] * block_cols + jnp.arange(block_cols, dtype=jnp.int32)[None, :]
    row_hit = (jnp.abs(rows_here[:, :, None] - stamp_r[:, None, :]) <= STAMP_HALF).astype(
        jnp.float32
    )
    col_hit = (jnp.abs(stamp_c[:, :, None] - cols_here[:, None, :]) <= STAMP_HALF).astype(
        jnp.float32
    )
    counts = jnp.einsum("nis,nsj->nij", row_hit, col_hit, precision=HIGH)
    return jnp.minimum(counts, 1.0)


def design_of(conv, info_rows, own_stamp_r, own_stamp_c, strip_rows, block_cols):
    row_start = info_rows[:, 0].astype(jnp.int32)
    blocks = info_rows[:, 1].astype(jnp.int32)
    live = info_rows[:, 2]

    def window_of(first_row, block):
        return lax.dynamic_slice(
            conv,
            (jnp.int32(0), first_row, block * block_cols),
            (conv.shape[0], strip_rows, block_cols),
        )

    windows = jax.vmap(window_of)(row_start, blocks)
    n_items = info_rows.shape[0]
    flattened = windows.reshape(n_items, windows.shape[1], -1)
    design = jnp.concatenate(
        [flattened, jnp.ones((n_items, 1, flattened.shape[2]), jnp.float32)], axis=1
    )
    stamp_r = jnp.broadcast_to(own_stamp_r[None, :], (n_items, own_stamp_r.shape[0]))
    stamp_c = jnp.broadcast_to(own_stamp_c[None, :], (n_items, own_stamp_c.shape[0]))
    weight = (
        stamp_mask(row_start, blocks, stamp_r, stamp_c, strip_rows, block_cols)
        * live[:, None, None]
    )
    weighted = design * weight.reshape(n_items, 1, -1)
    return (design, weighted)


def factor_of(design, weighted, capacity):
    n_items = design.shape[0]
    columns = design.shape[1]
    normal = jnp.einsum("skp,slp->skl", weighted, design, precision=HIGH)
    pair_normal = normal.reshape(n_items // capacity, capacity, columns, columns).sum(axis=1)
    pair_normal = pair_normal + RIDGE * jnp.eye(columns, dtype=jnp.float32)
    return jnp.linalg.cholesky(pair_normal)


def finish_fit(design, weighted, factor, pixels, capacity):
    n_items = design.shape[0]
    columns = design.shape[1]
    values = pixels.reshape(n_items, -1)
    moment = jnp.einsum("skp,sp->sk", weighted, values, precision=HIGH)
    pair_moment = moment.reshape(n_items // capacity, capacity, columns).sum(axis=1)
    inner = lax.linalg.triangular_solve(factor, pair_moment[..., None], left_side=True, lower=True)
    coefficients = lax.linalg.triangular_solve(
        factor, inner, left_side=True, lower=True, transpose_a=True
    )[..., 0]
    slot_coeff = jnp.repeat(coefficients, capacity, axis=0)
    model_image = jnp.einsum("skp,sk->sp", design, slot_coeff, precision=HIGH)
    return (values - model_image).reshape(pixels.shape)


def on_device(
    template, science, dest, row_offset, col_block, basis_rows, basis_cols, stamp_rows, stamp_cols
):
    peers = lax.axis_size("patch")
    own_index = lax.axis_index("patch")
    half_taps = (basis_rows.shape[1] - 1) // 2
    strips, strip_rows, block_cols = science.shape
    capacity = CAP
    slots = peers * capacity
    group_pairs = math.gcd(peers, 16)
    n_groups = peers // group_pairs
    per_group = group_pairs * capacity
    haloed = with_halo(template, (("patch", 1),), half_taps)
    framed = jnp.pad(haloed, ((half_taps, half_taps), (0, 0)))
    targets = dest[:, 0]
    strip_order = jnp.arange(strips, dtype=jnp.int32)
    earlier = (targets[:, None] == targets[None, :]) & (strip_order[None, :] < strip_order[:, None])
    rank_of = jnp.sum(earlier.astype(jnp.int32), axis=1)
    slot_of = targets * capacity + rank_of
    slot_ids = jnp.arange(slots, dtype=jnp.int32)
    slot_hot = (slot_ids[:, None] == slot_of[None, :]).astype(jnp.float32)
    strip_hot = (slot_of[:, None] == slot_ids[None, :]).astype(jnp.float32)
    positions = jnp.stack([row_offset, col_block, jnp.ones_like(row_offset)], axis=1).astype(
        jnp.float32
    )
    slot_info = jnp.dot(slot_hot, positions, precision=HIGH)
    outgoing = jnp.dot(slot_hot, science.reshape(strips, -1), precision=HIGH).reshape(
        slots, strip_rows, block_cols
    )
    own_stamp_r = lax.dynamic_index_in_dim(stamp_rows, own_index, 0, keepdims=False)
    own_stamp_c = lax.dynamic_index_in_dim(stamp_cols, own_index, 0, keepdims=False)
    arrived, arrived_info = (
        lax.all_to_all(outgoing, "patch", split_axis=0, concat_axis=0, tiled=True),
        lax.all_to_all(slot_info, "patch", split_axis=0, concat_axis=0, tiled=True),
    )

    def one_basis(row_taps, col_taps):
        return filter_field(framed, row_taps, col_taps)

    conv = jax.vmap(one_basis)(basis_rows, basis_cols)

    def fit_group(group):
        pixels, info_rows = group
        design, weighted = design_of(
            conv, info_rows, own_stamp_r, own_stamp_c, strip_rows, block_cols
        )
        factor = factor_of(design, weighted, capacity)
        return finish_fit(design, weighted, factor, pixels, capacity)

    grouped = lax.map(
        fit_group,
        (
            arrived.reshape(n_groups, per_group, strip_rows, block_cols),
            arrived_info.reshape(n_groups, per_group, 3),
        ),
    )
    residuals = grouped.reshape(slots, strip_rows, block_cols)
    returned = lax.all_to_all(residuals, "patch", split_axis=0, concat_axis=0, tiled=True)
    picked = jnp.dot(strip_hot, returned.reshape(slots, -1), precision=HIGH)
    return picked.reshape(strips, strip_rows, block_cols)


def solution(mesh):
    placed = (
        P(None, ("groups", "patch")),
        P(("groups", "patch"), None, None),
        P(("groups", "patch"), None),
        P(("groups", "patch")),
        P(("groups", "patch")),
        P(),
        P(),
        P("groups", None),
        P("groups", None),
    )
    return jax.shard_map(
        on_device,
        mesh=mesh,
        in_specs=placed,
        out_specs=P(("groups", "patch"), None, None),
        check_vma=False,
    )
```

profile of v0, /device:TPU:0, one launch (start us, length us, event | category | flops | bytes accessed | tf_op | source)
XLA Modules:
  0.0 338.4 jit_solution(11568813379290508286)
XLA Ops:
  0.8 2.4 collective-permute-start
  6.2 1.5 fusion.49
  7.7 9.3 %all-to-all-start.1 = ((f32[16,2,3]{2,1,0:T(2,128)}), f32[16,2,3]{2,1,0:T(2,128)S(1)}, u32[]{:S(2)}, u32[]{:S(2)}) async-start(f32[16,2,3]{2,1,0:T(2,128)} %bitcast.50), calls=%async_computation.1 | async-start | bytes 32768 | tf_op jit(solution)/shard_map/all_to_all | solution.py:144
  23.5 5.5 %all-to-all-start = ((f32[32,4,128]{2,1,0:T(4,128)}), f32[32,4,128]{2,1,0:T(4,128)S(1)}, u32[]{:S(2)}, u32[]{:S(2)}) async-start(f32[32,4,128]{2,1,0:T(4,128)} %copy.40), calls=%async_computation | async-start | bytes 131072 | tf_op jit(solution)/shard_map/all_to_all | solution.py:143
  31.1 1.6 pad_slice_fusion.20
  32.9 19.8 %multiply_add_fusion = f32[27,84,1024]{2,1,0:T(8,128)} fusion(f32[84,1024]{1,0:T(8,128)S(1)} %get-tuple-element.64, f32[27]{0:T(128)S(1)} %get-tuple-element.111, f32[84,1024]{1,0:T(8,128)S(1)} %get-tuple-element.63, f32[27]{0:T(128)S(1)} %get-tuple-element.110, f32[84,1024]{1,0:T(8,128)S(1)} %get-tuple-element.62, f32[27]{0:T(128)S(1)} %get-tuple-element.92, ...), kind=kLoop, calls=%fused_computation.2 | loop fusion | flops 95219712 | bytes 16517340 | tf_op jit(solution)/shard_map/vmap()/add | solution.py:39
  52.7 73.2 %fusion = f32[27,64,1024]{2,1,0:T(8,128)} fusion(f32[27,84,1024]{2,1,0:T(8,128)} %multiply_add_fusion, f32[27]{0:T(128)S(1)} %get-tuple-element.90, f32[27]{0:T(128)S(1)} %get-tuple-element.89, f32[27]{0:T(128)S(1)} %get-tuple-element.71, f32[27]{0:T(128)S(1)} %get-tuple-element.72, f32[27]{0:T(128)S(1)} %get-tuple-element.73, f32[27]{0:T(128)S(1)} %get-tuple-element.74, ...), kind=kLoop, calls=%fused_computation.4 | loop fusion | flops 72548352 | bytes 155715808 | tf_op jit(solution)/shard_map/vmap()/add | solution.py:42
  125.9 113.3 %while.1 = (s32[]{:T(128)}, f32[27,64,1024]{2,1,0:T(8,128)}, s32[32,3]{0,1:T(4,128)S(1)}, f32[32,27,4,128]{3,2,1,0:T(4,128)}, s32[]{:T(128)}) while((s32[]{:T(128)}, f32[27,64,1024]{2,1,0:T(8,128)}, s32[32,3]{0,1:T(4,128)S(1)}, f32[32,27,4,128]{3,2,1,0:T(4,128)}, s32[]{:T(128)}) %tuple.85), condition=%wide.while_cond, body=%wide.while_body.sunk | while | flops 2 | bytes 112233 | solution.py:65
  126.5 2.9 bitcast_dynamic-update-slice_fusion.2
  130.0 3.0 bitcast_dynamic-update-slice_fusion.2
  133.6 3.0 bitcast_dynamic-update-slice_fusion.2
  137.1 3.0 bitcast_dynamic-update-slice_fusion.2
  140.7 3.0 bitcast_dynamic-update-slice_fusion.2
  144.2 3.0 bitcast_dynamic-update-slice_fusion.2
  147.8 2.9 bitcast_dynamic-update-slice_fusion.2
  151.3 3.0 bitcast_dynamic-update-slice_fusion.2
  154.9 2.9 bitcast_dynamic-update-slice_fusion.2
  158.4 3.0 bitcast_dynamic-update-slice_fusion.2
  161.9 3.0 bitcast_dynamic-update-slice_fusion.2
  165.5 3.0 bitcast_dynamic-update-slice_fusion.2
  169.0 2.9 bitcast_dynamic-update-slice_fusion.2
  172.5 3.0 bitcast_dynamic-update-slice_fusion.2
  176.0 3.0 bitcast_dynamic-update-slice_fusion.2
  179.6 3.0 bitcast_dynamic-update-slice_fusion.2
  183.2 3.0 bitcast_dynamic-update-slice_fusion.2
  186.7 3.0 bitcast_dynamic-update-slice_fusion.2
  190.3 2.9 bitcast_dynamic-update-slice_fusion.2
  193.7 3.0 bitcast_dynamic-update-slice_fusion.2
  197.3 3.0 bitcast_dynamic-update-slice_fusion.2
  200.8 3.0 bitcast_dynamic-update-slice_fusion.2
  204.4 3.0 bitcast_dynamic-update-slice_fusion.2
  207.9 3.0 bitcast_dynamic-update-slice_fusion.2
  211.5 3.0 bitcast_dynamic-update-slice_fusion.2
  215.0 2.9 bitcast_dynamic-update-slice_fusion.2
  218.6 3.0 bitcast_dynamic-update-slice_fusion.2
  222.1 3.0 bitcast_dynamic-update-slice_fusion.2
  225.7 3.0 bitcast_dynamic-update-slice_fusion.2
  229.2 3.0 bitcast_dynamic-update-slice_fusion.2
  232.8 3.0 bitcast_dynamic-update-slice_fusion.2
  236.3 2.9 bitcast_dynamic-update-slice_fusion.2
  239.3 2.0 reshape.238
  241.3 2.1 bitcast_reduce_fusion
  243.6 41.0 %custom-call.11 = f32[16,28,28]{2,1,0:T(8,128)S(1)} custom-call(f32[16,28,28]{2,1,0:T(8,128)S(1)} %fusion.35), custom_call_target="Cholesky" | custom-call | tf_op jit(solution)/shard_map/while/body/eval_jaxpr/jit(cholesky)/cholesky | solution.py:93
  284.9 34.7 %custom-call.12 = f32[16,1,28,28]{2,3,1,0:T(8,128)S(1)} custom-call(f32[16,1,28,28]{3,2,1,0:T(8,128)S(1)} %select_bitcast_fusion), custom_call_target="InvertDiagBlocksLowerTriangular" | custom-call | tf_op jit(solution)/shard_map/while/body/eval_jaxpr/triangular_solve | solution.py:103
  319.7 2.0 fusion.20
  322.6 1.4 fusion.24
  324.7 6.0 %all-to-all-start.2 = ((f32[32,4,128]{2,1,0:T(4,128)}), f32[32,4,128]{2,1,0:T(4,128)S(1)}, u32[]{:S(2)}, u32[]{:S(2)}) async-start(f32[32,4,128]{2,1,0:T(4,128)} %reshape.203), calls=%async_computation.2 | async-start | bytes 131072 | tf_op jit(solution)/shard_map/all_to_all | solution.py:168
  330.7 6.9 %all-to-all-done.2 = f32[32,4,128]{2,1,0:T(4,128)S(1)} async-done(((f32[32,4,128]{2,1,0:T(4,128)}), f32[32,4,128]{2,1,0:T(4,128)S(1)}, u32[]{:S(2)}, u32[]{:S(2)}) %all-to-all-start.2) | async-done | bytes 65568 | tf_op jit(solution)/shard_map/all_to_all | solution.py:168
  (114 shorter events, 34.2 us)
Async XLA Ops:
  0.8 29.0 %collective-permute-start = (f32[64,10]{1,0:T(8,128)S(1)}, f32[64,10]{1,0:T(8,128)S(1)}, u32[]{:S(2)}, u32[]{:S(2)}) collective-permute-start(f32[64,10]{1,0:T(8,128)S(1)} %get-tuple-element.66), channel_id=1, source_target_pairs={{0,1},{1,2},{2,3},{3,4},{4,5},{5,6},{6,7},{7,8},{8,9},{9,10},{10,1... | collective-permute-start | bytes 7688 | tf_op jit(solution)/shard_map/ppermute | solution.py:24
  3.2 26.7 %collective-permute-start.1 = (f32[64,10]{1,0:T(8,128)S(1)}, f32[64,10]{1,0:T(8,128)S(1)}, u32[]{:S(2)}, u32[]{:S(2)}) collective-permute-start(f32[64,10]{1,0:T(8,128)S(1)} %get-tuple-element.65), channel_id=1, source_target_pairs={{1,0},{2,1},{3,2},{4,3},{5,4},{6,5},{7,6},{8,7},{9,8},{10,9},{11,1... | collective-permute-start | bytes 7688 | tf_op jit(solution)/shard_map/ppermute | solution.py:26
  7.7 15.8 %all-to-all-start.1 = ((f32[16,2,3]{2,1,0:T(2,128)}), f32[16,2,3]{2,1,0:T(2,128)S(1)}, u32[]{:S(2)}, u32[]{:S(2)}) async-start(f32[16,2,3]{2,1,0:T(2,128)} %bitcast.50), calls=%async_computation.1 | async-start | bytes 32768 | tf_op jit(solution)/shard_map/all_to_all | solution.py:144
  23.5 296.2 %all-to-all-start = ((f32[32,4,128]{2,1,0:T(4,128)}), f32[32,4,128]{2,1,0:T(4,128)S(1)}, u32[]{:S(2)}, u32[]{:S(2)}) async-start(f32[32,4,128]{2,1,0:T(4,128)} %copy.40), calls=%async_computation | async-start | bytes 131072 | tf_op jit(solution)/shard_map/all_to_all | solution.py:143
  239.3 91.4 %copy-start = (s32[16,1]{0,1:T(1,128)S(1)}, s32[16,1]{0,1:T(1,128)}, u32[]{:S(2)}) copy-start(s32[16,1]{0,1:T(1,128)} %param.11) | copy-start | bytes 196
  324.7 12.9 %all-to-all-start.2 = ((f32[32,4,128]{2,1,0:T(4,128)}), f32[32,4,128]{2,1,0:T(4,128)S(1)}, u32[]{:S(2)}, u32[]{:S(2)}) async-start(f32[32,4,128]{2,1,0:T(4,128)} %reshape.203), calls=%async_computation.2 | async-start | bytes 131072 | tf_op jit(solution)/shard_map/all_to_all | solution.py:168
where the time goes:
time: 341 us; the launch traced here: 338 us
  other arithmetic  171 us (50%)
  local copies, waits for them, and re-layouts  126 us (37%)
  starting transfers between devices  24.5 us (7%)
  matrix products  9.49 us (3%)
  waiting for transfers between devices  7.36 us (2%)
    gather x96, local copies, waits for them, and re-layouts  113 us
    add x1, other arithmetic, filter_field(): result + row_taps[shift_tap] * across[shift_tap:shift_tap + out_rows, :]  73.2 us
    another operation x4, other arithmetic, factor_of(): return jnp.linalg.cholesky(pair_normal)  41.2 us
    another operation x3, other arithmetic, finish_fit(): lax.linalg.triangular_solve(factor, inner, left_side=True, lower=True, tr...  34.8 us
    add x1, other arithmetic, filter_field(): across + col_taps[shift_tap] * padded[:, shift_tap:shift_tap + out_cols]  19.8 us
    all_to_all x1, starting transfers between devices, on_device(): lax.all_to_all(slot_info, 'patch', split_axis=0, concat_axis=0, tiled=True)  9.3 us
    all_to_all x1, waiting for transfers between devices, on_device(): lax.all_to_all(residuals, 'patch', split_axis=0, concat_axis=0, tiled=True)  6.87 us
  transfers between devices with their start and end apart: 5, of which 2 were waited for; matrix products, arithmetic and copies ran while one was open for 89% of the time, Pallas kernels for 0%

commit v1 on v0

v1 whole, which is shorter than its diff:
```python
import functools
import math

import jax
import jax.numpy as jnp
from jax import lax
from jax.experimental import pallas as pl
from jax.experimental.pallas import tpu as pltpu
from jax.sharding import PartitionSpec as P

CAP = 2
STAMP_HALF = 10
RIDGE = 1.0
HIGH = lax.Precision.HIGHEST
F32 = jnp.float32
BF16 = jnp.bfloat16


def up(value, unit):
    return -(-value // unit) * unit


def split_in_two(values):
    high = values.astype(BF16)
    return high, (values - high.astype(F32)).astype(BF16)


def with_halo(cells, sides, width):
    for axis, dim in sides:
        count = lax.axis_size(axis)
        ends = count - 1
        head = lax.slice_in_dim(cells, 0, width, axis=dim)
        tail = lax.slice_in_dim(cells, cells.shape[dim] - width, cells.shape[dim], axis=dim)
        cells = jnp.concatenate(
            [
                lax.ppermute(tail, axis, [(i, (i + 1) % count) for i in range(ends)]),
                cells,
                lax.ppermute(head, axis, [((i + 1) % count, i) for i in range(ends)]),
            ],
            axis=dim,
        )
    return cells


def contract_last(left, right):
    return lax.dot_general(left, right, (((1,), (1,)), ((), ())), preferred_element_type=F32)


def fit_kernel(
    strip_rows,
    pos_ref,
    stamp_r_ref,
    stamp_c_ref,
    framed_ref,
    pixels_ref,
    rows_ref,
    cols_ref,
    out_ref,
    row_taps_ref,
    row_bands_ref,
    col_bands_ref,
    across_ref,
    design_ref,
    gram_ref,
):
    bases, taps = rows_ref.shape
    lanes = pixels_ref.shape[1]
    pair_rows = CAP * strip_rows
    n_rows = pixels_ref.shape[0]
    pairs = n_rows // pair_rows
    stamps = stamp_r_ref.shape[1]
    columns = bases + 1
    padded = up(columns + 1, 8)
    part = 2 * lanes // 4
    pitch = part // CAP
    step = pl.program_id(0)
    me = lax.axis_index("patch")

    @pl.when(step == 0)
    def _():
        sub = lax.broadcasted_iota(jnp.int32, (pair_rows, lanes), 0)
        wide_sub = lax.broadcasted_iota(jnp.int32, (lanes, lanes), 0)
        wide_lane = lax.broadcasted_iota(jnp.int32, (lanes, lanes), 1)
        row_taps_ref[...] = jnp.zeros_like(row_taps_ref)
        for k in range(bases):
            tap_row = jnp.concatenate(
                [rows_ref[k : k + 1, :], jnp.zeros((1, lanes - taps), F32)], axis=1
            )
            spread = pltpu.roll(
                jnp.broadcast_to(tap_row, (pair_rows, lanes)), 0, 1, stride=1, stride_axis=0
            )
            spread = jnp.where(sub < strip_rows, spread, pltpu.roll(spread, pitch - strip_rows, 1))
            row_taps_ref[pl.ds(k * pair_rows, pair_rows), :] = spread
            tap_col = jnp.concatenate(
                [cols_ref[k : k + 1, :], jnp.zeros((1, lanes - taps), F32)], axis=1
            )
            band = pltpu.roll(
                jnp.broadcast_to(tap_col, (lanes, lanes)), 0, 1, stride=1, stride_axis=0
            )
            for side in range(2):
                keep = wide_lane >= wide_sub if side == 0 else wide_lane < wide_sub
                high, low = split_in_two(jnp.where(keep, band, 0.0))
                col_bands_ref[k, 0:lanes, pl.ds(side * lanes, lanes)] = high
                col_bands_ref[k, lanes : 2 * lanes, pl.ds(side * lanes, lanes)] = low
        taps_f32 = row_taps_ref[...]
        taps_f32 = taps_f32 + pltpu.roll(taps_f32, part, 1)
        high, low = split_in_two(taps_f32)
        row_bands_ref[:, 0:lanes] = high
        row_bands_ref[:, lanes : 2 * lanes] = low

    for p in range(pairs):
        windows = []
        for c in range(CAP):
            slot = step * (pairs * CAP) + p * CAP + c
            first = pos_ref[slot, 0]
            block = pos_ref[slot, 1]
            over = lax.rem(first, 8)
            loaded = framed_ref[
                pl.ds(pl.multiple_of(first - over, 8), pitch + 8),
                pl.ds(pl.multiple_of(block * lanes, lanes), 2 * lanes),
            ]
            loaded = pltpu.roll(loaded, lax.rem(pitch + 8 - over, pitch + 8), 0)
            windows.append(loaded[:pitch])
        high, low = split_in_two(jnp.concatenate(windows, axis=0))
        stacked = jnp.concatenate([high, low, high, low], axis=0)
        across = jnp.dot(row_bands_ref[...], stacked, preferred_element_type=F32)
        for k in range(bases):
            across_ref[k, pl.ds(p * pair_rows, pair_rows), :] = across[
                k * pair_rows : (k + 1) * pair_rows, :
            ]

    for k in range(bases):
        high, low = split_in_two(across_ref[k])
        product = contract_last(jnp.concatenate([high, low], axis=0), col_bands_ref[k])
        product = product[:n_rows] + product[n_rows:]
        design_ref[pl.ds(k * n_rows, n_rows), :] = product[:, :lanes] + product[:, lanes:]
    design_ref[pl.ds(bases * n_rows, n_rows), :] = jnp.ones((n_rows, lanes), F32)
    design_ref[pl.ds(columns * n_rows, n_rows), :] = pixels_ref[...]
    for k in range(columns + 1, padded):
        design_ref[pl.ds(k * n_rows, n_rows), :] = jnp.zeros((n_rows, lanes), F32)

    sub = lax.broadcasted_iota(jnp.int32, (pair_rows, lanes), 0)
    lane = lax.broadcasted_iota(jnp.int32, (pair_rows, lanes), 1)
    for p in range(pairs):
        slot = step * (pairs * CAP) + p * CAP
        row_at = jnp.where(sub < strip_rows, pos_ref[slot, 0], pos_ref[slot + 1, 0] - strip_rows)
        col_at = jnp.where(sub < strip_rows, pos_ref[slot, 1], pos_ref[slot + 1, 1])
        live = jnp.where(sub < strip_rows, pos_ref[slot, 2], pos_ref[slot + 1, 2])
        row_at = (row_at + sub).astype(F32)
        col_at = (col_at * lanes + lane).astype(F32)
        nearest = jnp.full((pair_rows, lanes), 1e9, F32)
        for m in range(stamps):
            row_gap = jnp.abs(row_at - stamp_r_ref[me, m].astype(F32))
            col_gap = jnp.abs(col_at - stamp_c_ref[me, m].astype(F32))
            nearest = jnp.minimum(nearest, jnp.maximum(row_gap, col_gap))
        weight = jnp.where((nearest <= STAMP_HALF) & (live > 0), 1.0, 0.0)
        pieces = []
        for q in range(pair_rows):
            design = design_ref[pl.ds(p * pair_rows + q, padded, stride=n_rows), :]
            pieces.append(design * weight[q : q + 1, :])
        high, low = split_in_two(jnp.concatenate(pieces, axis=1))
        both = jnp.concatenate([high, low], axis=0)
        gram = contract_last(both, both)
        gram_ref[pl.ds(p * padded, padded), 0 : 2 * padded] = gram[:padded] + gram[padded:]

    tiles = padded // 8
    sub8 = lax.broadcasted_iota(jnp.int32, (8, pairs), 0)
    system = []
    for k in range(columns):
        turned = gram_ref[pl.ds(k, pairs, stride=padded), 0 : 2 * padded].T
        turned = turned[:padded] + turned[padded:]
        row = [turned[8 * t : 8 * t + 8] for t in range(tiles)]
        row[k // 8] = row[k // 8] + jnp.where(sub8 == k % 8, RIDGE, 0.0)
        system.append(row)
    for n in range(columns):
        at, within = n // 8, n % 8
        inverse = 1.0 / system[n][at][within : within + 1, :]
        pivot = [system[n][t] * inverse for t in range(at, tiles)]
        for k in range(columns):
            if k != n:
                factor = system[k][at][within : within + 1, :]
                for t in range(at, tiles):
                    system[k][t] = system[k][t] - factor * pivot[t - at]
        system[n][at:] = pivot
    at, within = columns // 8, columns % 8
    coeff = jnp.concatenate(
        [system[k][at][within : within + 1, :] for k in range(columns)]
        + [jnp.zeros((padded - columns, pairs), F32)],
        axis=0,
    ).T
    coeff = jnp.broadcast_to(coeff[:, None, :], (pairs, pair_rows, padded)).reshape(n_rows, padded)
    rest = pixels_ref[...]
    for k in range(columns):
        rest = rest - design_ref[pl.ds(k * n_rows, n_rows), :] * coeff[:, k : k + 1]
    out_ref[...] = rest


def fit(framed, pixels, positions, stamp_r, stamp_c, basis_rows, basis_cols, strip_rows):
    bases = basis_rows.shape[0]
    lanes = pixels.shape[1]
    slots = positions.shape[0]
    pair_rows = CAP * strip_rows
    pairs = math.gcd(slots // CAP, 16)
    n_rows = pairs * pair_rows
    padded = up(bases + 2, 8)
    even = up(bases, 2)
    smem = pl.BlockSpec(memory_space=pltpu.SMEM)
    whole = pl.BlockSpec(memory_space=pltpu.VMEM)
    block = pl.BlockSpec((n_rows, lanes), lambda i: (i, 0))
    return pl.pallas_call(
        functools.partial(fit_kernel, strip_rows),
        grid=(pixels.shape[0] // n_rows,),
        out_shape=jax.ShapeDtypeStruct(pixels.shape, F32),
        in_specs=[smem, smem, smem, whole, block, whole, whole],
        out_specs=block,
        scratch_shapes=[
            pltpu.VMEM((even * pair_rows, lanes), F32),
            pltpu.VMEM((even * pair_rows, 2 * lanes), BF16),
            pltpu.VMEM((bases, 2 * lanes, 2 * lanes), BF16),
            pltpu.VMEM((bases, n_rows, 2 * lanes), F32),
            pltpu.VMEM((padded * n_rows, lanes), F32),
            pltpu.VMEM((pairs * padded, lanes), F32),
        ],
        compiler_params=pltpu.CompilerParams(vmem_limit_bytes=48 << 20),
    )(positions, stamp_r, stamp_c, framed, pixels, basis_rows, basis_cols)


def on_device(
    template, science, dest, row_offset, col_block, basis_rows, basis_cols, stamp_rows, stamp_cols
):
    peers = lax.axis_size("patch")
    half_taps = (basis_rows.shape[1] - 1) // 2
    strips, strip_rows, block_cols = science.shape
    slots = peers * CAP
    haloed = with_halo(template, (("patch", 1),), half_taps)
    window = block_cols // 2 // CAP
    framed = jnp.pad(
        haloed,
        (
            (half_taps, window + 8 - strip_rows - half_taps),
            (0, block_cols - 2 * half_taps),
        ),
    )
    targets = dest[:, 0]
    strip_order = jnp.arange(strips, dtype=jnp.int32)
    earlier = (targets[:, None] == targets[None, :]) & (strip_order[None, :] < strip_order[:, None])
    rank_of = jnp.sum(earlier.astype(jnp.int32), axis=1)
    slot_of = targets * CAP + rank_of
    slot_ids = jnp.arange(slots, dtype=jnp.int32)
    slot_hot = (slot_ids[:, None] == slot_of[None, :]).astype(F32)
    strip_hot = (slot_of[:, None] == slot_ids[None, :]).astype(F32)
    positions = jnp.stack([row_offset, col_block, jnp.ones_like(row_offset)], axis=1).astype(F32)
    slot_info = jnp.dot(slot_hot, positions, precision=HIGH)
    outgoing = jnp.dot(slot_hot, science.reshape(strips, -1), precision=HIGH).reshape(
        slots, strip_rows, block_cols
    )
    arrived, arrived_info = (
        lax.all_to_all(outgoing, "patch", split_axis=0, concat_axis=0, tiled=True),
        lax.all_to_all(slot_info, "patch", split_axis=0, concat_axis=0, tiled=True),
    )
    residuals = fit(
        framed,
        arrived.reshape(slots * strip_rows, block_cols),
        arrived_info.astype(jnp.int32),
        stamp_rows,
        stamp_cols,
        basis_rows,
        basis_cols,
        strip_rows,
    ).reshape(slots, strip_rows, block_cols)
    returned = lax.all_to_all(residuals, "patch", split_axis=0, concat_axis=0, tiled=True)
    picked = jnp.dot(strip_hot, returned.reshape(slots, -1), precision=HIGH)
    return picked.reshape(strips, strip_rows, block_cols)


def solution(mesh):
    placed = (
        P(None, ("groups", "patch")),
        P(("groups", "patch"), None, None),
        P(("groups", "patch"), None),
        P(("groups", "patch")),
        P(("groups", "patch")),
        P(),
        P(),
        P("groups", None),
        P("groups", None),
    )
    return jax.shard_map(
        on_device,
        mesh=mesh,
        in_specs=placed,
        out_specs=P(("groups", "patch"), None, None),
        check_vma=False,
    )
```

time: 341 us -> 50.6 us (0.15)
  other arithmetic: 171 us -> 0.2 us
  local copies, waits for them, and re-layouts: 126 us -> 3.88 us
  matrix products: 9.49 us -> 1.35 us
  waiting for transfers between devices: 7.36 us -> 15 us
  Pallas kernels: 0 us -> 7.33 us
    gather x96 -> x0, local copies, waits for them, and re-layouts: 113 us -> none
    add x6 -> x1, other arithmetic: 93.8 us -> 0.01 us  [on_device(): slot_of = targets * CAP + rank_of]
    another operation x7 -> x0, other arithmetic: 76 us -> none  [the longest x4 41.2 us: factor_of(): return jnp.linalg.cholesky(pair_normal)]
    pallas_call x0 -> x1, Pallas kernels: none -> 7.33 us  [fit(): pl.pallas_call(functools.partial(fit_kernel, strip_rows), grid=(pixels.sh...]
    dot_general x4 -> x0, matrix products: 5.85 us -> none  [the longest x1 2.11 us: factor_of(): normal = jnp.einsum('skp,slp->skl', weighted, design, precision=HIGH)]
    all_to_all x1, waiting for transfers between devices: 0.48 us -> 5.53 us  [on_device(): lax.all_to_all(slot_info, 'patch', split_axis=0, concat_axis=0, tiled=True)]
    mul x4 -> x0, local copies, waits for them, and re-layouts: 3.54 us -> none  [the longest x2 1.77 us: filter_field(): col_taps[shift_tap] * padded[:, shift_tap:shift_tap + out_cols]]
  transfers between devices with their start and end apart: 5 -> 5, of which waited for: 2 -> 4; matrix products, arithmetic and copies ran while one was open for 89% -> 3% of each run, Pallas kernels for 0% -> 0%
where the time goes in v1:
time: 50.6 us; the launch traced here: 50.1 us
  starting transfers between devices  22.2 us (44%)
  waiting for transfers between devices  15 us (30%)
  Pallas kernels  7.33 us (14%)
  local copies, waits for them, and re-layouts  3.88 us (8%)
  matrix products  1.35 us (3%)
    all_to_all x1, starting transfers between devices, on_device(): lax.all_to_all(residuals, 'patch', split_axis=0, concat_axis=0, tiled=True)  7.85 us
    all_to_all x1, starting transfers between devices, on_device(): lax.all_to_all(slot_info, 'patch', split_axis=0, concat_axis=0, tiled=True)  7.39 us
    pallas_call x1, Pallas kernels, fit(): pl.pallas_call(functools.partial(fit_kernel, strip_rows), grid=(pixels.sh...  7.33 us
    all_to_all x1, waiting for transfers between devices, on_device(): lax.all_to_all(residuals, 'patch', split_axis=0, concat_axis=0, tiled=True)  6.88 us
    all_to_all x1, waiting for transfers between devices, on_device(): lax.all_to_all(slot_info, 'patch', split_axis=0, concat_axis=0, tiled=True)  5.53 us
    all_to_all x1, starting transfers between devices, on_device(): lax.all_to_all(outgoing, 'patch', split_axis=0, concat_axis=0, tiled=True)  3.49 us
    ppermute x1, waiting for transfers between devices, with_halo(): lax.ppermute(head, axis, [((i + 1) % count, i) for i in range(ends)])  2.54 us
    ppermute x1, starting transfers between devices, with_halo(): lax.ppermute(tail, axis, [(i, (i + 1) % count) for i in range(ends)])  2.18 us
  transfers between devices with their start and end apart: 5, of which 4 were waited for; matrix products, arithmetic and copies ran while one was open for 3% of the time, Pallas kernels for 0%

profile of v1, /device:TPU:0, one launch (start us, length us, event | category | flops | bytes accessed | tf_op | source)
XLA Modules:
  0.0 50.1 jit_solution(17253542308550014877)
XLA Ops:
  0.0 0.0 copy-start.8
  0.0 0.7 %copy-done.8 = s32[16,1]{0,1:T(1,128)S(1)} copy-done((s32[16,1]{0,1:T(1,128)S(1)}, s32[16,1]{0,1:T(1,128)}, u32[]{:S(2)}) %copy-start.8) | copy-done | bytes 88
  0.7 0.2 convert_reduce_fusion
  0.8 0.0 copy-start.6
  0.9 0.0 copy-start.7
  0.9 0.1 pad.7.clone
  0.9 0.0 copy-start.3
  0.9 0.0 copy-start.2
  0.9 0.6 %copy-done.6 = s32[16]{0:T(128)S(1)} copy-done((s32[16]{0:T(128)S(1)}, s32[16]{0:T(128)}, u32[]{:S(2)}) %copy-start.6) | copy-done | bytes 88
  1.5 0.0 copy-done.7
  1.5 0.9 %fusion.7 = f32[32,3]{1,0:T(8,128)} fusion(s32[16]{0:T(128)S(1)} %multiply_add_fusion, s32[16,1]{0,1:T(1,128)S(1)} %bitcast.51, s32[16,1]{0,1:T(1,128)S(1)} %bitcast.52, s32[3]{0:T(128)S(1)} %pad.7.clone), kind=kOutput, calls=%fused_computation.10 | convolution fusion | flops 19088 | bytes 588 | tf_op jit(solution)/shard_map/all_to_all | solution.py:259
  2.4 7.4 %all-to-all-start = ((f32[16,2,3]{2,1,0:T(2,128)}), f32[16,2,3]{2,1,0:T(2,128)S(1)}, u32[]{:S(2)}, u32[]{:S(2)}) async-start(f32[16,2,3]{2,1,0:T(2,128)} %bitcast.6), calls=%async_computation | async-start | bytes 32768 | tf_op jit(solution)/shard_map/all_to_all | solution.py:259
  9.8 0.0 copy-done.3
  9.8 0.3 fusion.3
  10.1 0.7 %copy.44 = f32[32,4,128]{2,1,0:T(4,128)} copy(f32[32,4,128]{2,0,1:T(8,128)S(1)} %fusion.3) | data formatting | bytes 131072 | tf_op jit(solution)/shard_map/dot_general | solution.py:254
  10.8 5.5 %all-to-all-done = f32[16,2,3]{2,1,0:T(2,128)S(1)} async-done(((f32[16,2,3]{2,1,0:T(2,128)}), f32[16,2,3]{2,1,0:T(2,128)S(1)}, u32[]{:S(2)}, u32[]{:S(2)}) %all-to-all-start) | async-done | bytes 416 | tf_op jit(solution)/shard_map/all_to_all | solution.py:259
  16.3 3.5 %all-to-all-start.1 = ((f32[32,4,128]{2,1,0:T(4,128)}), f32[32,4,128]{2,1,0:T(4,128)S(1)}, u32[]{:S(2)}, u32[]{:S(2)}) async-start(f32[32,4,128]{2,1,0:T(4,128)} %copy.44), calls=%async_computation.1 | async-start | bytes 131072 | tf_op jit(solution)/shard_map/all_to_all | solution.py:258
  19.8 0.0 copy-done.2
  19.8 0.0 copy-start.4
  19.8 0.1 fusion.21
  19.9 2.2 %collective-permute-start = (f32[64,10]{1,0:T(8,128)S(1)}, f32[64,10]{1,0:T(8,128)S(1)}, u32[]{:S(2)}, u32[]{:S(2)}) collective-permute-start(f32[64,10]{1,0:T(8,128)S(1)} %get-tuple-element.6), channel_id=1, source_target_pairs={{0,1},{1,2},{2,3},{3,4},{4,5},{5,6},{6,7},{7,8},{8,9},{9,10},{10,1... | collective-permute-start | bytes 7688 | tf_op jit(solution)/shard_map/ppermute | solution.py:36
  22.1 0.0 copy-start.5
  22.1 1.3 %collective-permute-start.1 = (f32[64,10]{1,0:T(8,128)S(1)}, f32[64,10]{1,0:T(8,128)S(1)}, u32[]{:S(2)}, u32[]{:S(2)}) collective-permute-start(f32[64,10]{1,0:T(8,128)S(1)} %get-tuple-element.5), channel_id=1, source_target_pairs={{1,0},{2,1},{3,2},{4,3},{5,4},{6,5},{7,6},{8,7},{9,8},{10,9},{11,1... | collective-permute-start | bytes 7688 | tf_op jit(solution)/shard_map/ppermute | solution.py:38
  23.4 0.0 copy-done.4
  23.4 0.1 copy.46.rows_ref
  23.5 0.0 copy-done.5
  23.5 0.1 copy.47.cols_ref
  23.6 0.1 copy.41
  23.7 0.1 copy.51
  23.8 0.0 collective-permute-done
  23.8 2.5 %collective-permute-done.1 = f32[64,10]{1,0:T(8,128)S(1)} collective-permute-done((f32[64,10]{1,0:T(8,128)S(1)}, f32[64,10]{1,0:T(8,128)S(1)}, u32[]{:S(2)}, u32[]{:S(2)}) %collective-permute-start.1) | collective-permute-done | bytes 2592 | tf_op jit(solution)/shard_map/ppermute | solution.py:38
  26.3 0.2 concatenate.3
  26.5 0.0 copy-start
  26.5 0.0 copy-start.1
  26.6 0.1 all-to-all-done.1
  26.6 0.6 %copy-done = s32[16,24]{1,0:T(8,128)S(1)} copy-done((s32[16,24]{1,0:T(8,128)S(1)}, s32[16,24]{1,0:T(8,128)}, u32[]{:S(2)}) %copy-start) | copy-done | bytes 1560
  27.2 0.0 copy-done.1
  27.2 7.3 %shard_map.91 = f32[128,128]{1,0:T(8,128)} custom-call(s32[32,3]{1,0:T(8,128)S(1)} %bitcast.48, s32[16,24]{1,0:T(8,128)S(1)} %copy-done, s32[16,24]{1,0:T(8,128)S(1)} %copy-done.1, f32[100,1152]{1,0:T(8,128)S(1)} %pad.4.framed_ref, f32[128,128]{1,0:T(8,128)S(1)} %bitcast.47, f32[27,21]{1,0:T(8,128)S(1)} %copy.46.rows_ref, f32[27,21]{1,0:T(8,128)S(1)} %copy.47.cols_ref), custom_call_target="tpu_custom_call" | custom-call | tf_op jit(solution)/shard_map/pallas_call | solution.py:210
  34.6 7.8 %all-to-all-start.2 = ((f32[32,4,128]{2,1,0:T(4,128)}), f32[32,4,128]{2,1,0:T(4,128)S(1)}, u32[]{:S(2)}, u32[]{:S(2)}) async-start(f32[32,4,128]{2,1,0:T(4,128)} %bitcast.11), calls=%async_computation.2 | async-start | bytes 131072 | tf_op jit(solution)/shard_map/all_to_all | solution.py:271
  42.4 6.9 %all-to-all-done.2 = f32[32,4,128]{2,1,0:T(4,128)S(1)} async-done(((f32[32,4,128]{2,1,0:T(4,128)}), f32[32,4,128]{2,1,0:T(4,128)S(1)}, u32[]{:S(2)}, u32[]{:S(2)}) %all-to-all-start.2) | async-done | bytes 65568 | tf_op jit(solution)/shard_map/all_to_all | solution.py:271
  49.3 0.2 fusion
  49.5 0.6 %copy.49 = f32[16,4,128]{2,1,0:T(4,128)} copy(f32[16,4,128]{2,0,1:T(8,128)S(1)} %fusion) | data formatting | bytes 65536 | tf_op jit(solution)/shard_map/dot_general | solution.py:272
  (4 shorter events, 0.1 us)
Async XLA Ops:
  0.0 0.7 %copy-start.8 = (s32[16,1]{0,1:T(1,128)S(1)}, s32[16,1]{0,1:T(1,128)}, u32[]{:S(2)}) copy-start(s32[16,1]{0,1:T(1,128)} %param.11) | copy-start | bytes 196
  0.8 0.7 %copy-start.6 = (s32[16]{0:T(128)S(1)}, s32[16]{0:T(128)}, u32[]{:S(2)}) copy-start(s32[16]{0:T(128)} %param.13) | copy-start | bytes 196
  0.9 0.7 %copy-start.7 = (s32[16]{0:T(128)S(1)}, s32[16]{0:T(128)}, u32[]{:S(2)}) copy-start(s32[16]{0:T(128)} %param.12) | copy-start | bytes 196
  0.9 8.8 %copy-start.3 = (f32[16,4,128]{2,1,0:T(4,128)S(1)}, f32[16,4,128]{2,1,0:T(4,128)}, u32[]{:S(2)}) copy-start(f32[16,4,128]{2,1,0:T(4,128)} %param.10) | copy-start | bytes 98308
  0.9 18.8 %copy-start.2 = (f32[64,1024]{1,0:T(8,128)S(1)}, f32[64,1024]{1,0:T(8,128)}, u32[]{:S(2)}) copy-start(f32[64,1024]{1,0:T(8,128)} %param.9) | copy-start | bytes 786436
  2.4 13.9 %all-to-all-start = ((f32[16,2,3]{2,1,0:T(2,128)}), f32[16,2,3]{2,1,0:T(2,128)S(1)}, u32[]{:S(2)}, u32[]{:S(2)}) async-start(f32[16,2,3]{2,1,0:T(2,128)} %bitcast.6), calls=%async_computation | async-start | bytes 32768 | tf_op jit(solution)/shard_map/all_to_all | solution.py:259
  16.3 10.4 %all-to-all-start.1 = ((f32[32,4,128]{2,1,0:T(4,128)}), f32[32,4,128]{2,1,0:T(4,128)S(1)}, u32[]{:S(2)}, u32[]{:S(2)}) async-start(f32[32,4,128]{2,1,0:T(4,128)} %copy.44), calls=%async_computation.1 | async-start | bytes 131072 | tf_op jit(solution)/shard_map/all_to_all | solution.py:258
  19.8 3.6 %copy-start.4 = (f32[27,21]{0,1:T(8,128)S(1)}, f32[27,21]{0,1:T(8,128)}, u32[]{:S(2)}) copy-start(f32[27,21]{0,1:T(8,128)} %param.14) | copy-start | bytes 6808
  19.9 3.9 %collective-permute-start = (f32[64,10]{1,0:T(8,128)S(1)}, f32[64,10]{1,0:T(8,128)S(1)}, u32[]{:S(2)}, u32[]{:S(2)}) collective-permute-start(f32[64,10]{1,0:T(8,128)S(1)} %get-tuple-element.6), channel_id=1, source_target_pairs={{0,1},{1,2},{2,3},{3,4},{4,5},{5,6},{6,7},{7,8},{8,9},{9,10},{10,1... | collective-permute-start | bytes 7688 | tf_op jit(solution)/shard_map/ppermute | solution.py:36
  22.1 1.4 %copy-start.5 = (f32[27,21]{0,1:T(8,128)S(1)}, f32[27,21]{0,1:T(8,128)}, u32[]{:S(2)}) copy-start(f32[27,21]{0,1:T(8,128)} %param.15) | copy-start | bytes 6808
  22.1 4.2 %collective-permute-start.1 = (f32[64,10]{1,0:T(8,128)S(1)}, f32[64,10]{1,0:T(8,128)S(1)}, u32[]{:S(2)}, u32[]{:S(2)}) collective-permute-start(f32[64,10]{1,0:T(8,128)S(1)} %get-tuple-element.5), channel_id=1, source_target_pairs={{1,0},{2,1},{3,2},{4,3},{5,4},{6,5},{7,6},{8,7},{9,8},{10,9},{11,1... | collective-permute-start | bytes 7688 | tf_op jit(solution)/shard_map/ppermute | solution.py:38
  26.5 0.7 %copy-start = (s32[16,24]{1,0:T(8,128)S(1)}, s32[16,24]{1,0:T(8,128)}, u32[]{:S(2)}) copy-start(s32[16,24]{1,0:T(8,128)} %stamp_r_ref.1) | copy-start | bytes 4612
  26.5 0.7 %copy-start.1 = (s32[16,24]{1,0:T(8,128)S(1)}, s32[16,24]{1,0:T(8,128)}, u32[]{:S(2)}) copy-start(s32[16,24]{1,0:T(8,128)} %stamp_c_ref.1) | copy-start | bytes 4612
  34.6 14.7 %all-to-all-start.2 = ((f32[32,4,128]{2,1,0:T(4,128)}), f32[32,4,128]{2,1,0:T(4,128)S(1)}, u32[]{:S(2)}, u32[]{:S(2)}) async-start(f32[32,4,128]{2,1,0:T(4,128)} %bitcast.11), calls=%async_computation.2 | async-start | bytes 131072 | tf_op jit(solution)/shard_map/all_to_all | solution.py:271

commit v2 on v0

v2 whole, which is shorter than its diff:
```python
import math

import jax
import jax.numpy as jnp
from jax import lax
from jax.experimental import pallas as pl
from jax.experimental.pallas import tpu as pltpu
from jax.sharding import PartitionSpec as P

CAP = 2
STAMP_HALF = 10
RIDGE = 1.0
HIGH = lax.Precision.HIGHEST
MESH = pl.DeviceIdType.MESH
F32 = jnp.float32
BF16 = jnp.bfloat16


def up(value, unit):
    return -(-value // unit) * unit


def split_in_two(values):
    high = values.astype(BF16)
    return high, (values - high.astype(F32)).astype(BF16)


def contract_last(left, right):
    return lax.dot_general(left, right, (((1,), (1,)), ((), ())), preferred_element_type=F32)


def exact_dot(left, right):
    return jnp.dot(left, right, precision=HIGH, preferred_element_type=F32)


def iota(shape, dim):
    return lax.broadcasted_iota(jnp.int32, shape, dim)


def routes_of(dest_ref, peers):
    strips = dest_ref.shape[0]
    slots = peers * CAP
    square = (strips, strips)
    down, across = iota(square, 0), iota(square, 1)
    target_down = jnp.broadcast_to(dest_ref[...], square)
    target_across = jnp.sum(jnp.where(down == across, target_down, 0), axis=0, keepdims=True)
    same = jnp.where(target_down == target_across, 1, 0)
    rank_down = jnp.sum(jnp.where(across < down, same, 0), axis=1, keepdims=True)
    rank_across = jnp.sum(jnp.where(down < across, same, 0), axis=0, keepdims=True)
    slot_down = target_down[:, 0:1] * CAP + rank_down
    slot_across = target_across * CAP + rank_across
    return slot_down == iota((strips, slots), 1), slot_across == iota((slots, strips), 0)


def build_bands(rows_ref, cols_ref, row_taps_ref, row_bands_ref, col_bands_ref, strip_rows):
    bases, taps = rows_ref.shape
    lanes = row_taps_ref.shape[1]
    pair_rows = CAP * strip_rows
    part = 2 * lanes // 4
    pitch = part // CAP
    sub = iota((pair_rows, lanes), 0)
    keep = iota((lanes, lanes), 1) >= iota((lanes, lanes), 0)
    row_taps_ref[...] = jnp.zeros_like(row_taps_ref)
    blank = jnp.zeros((1, lanes - taps), F32)

    def one_basis(k, carry):
        tap_row = jnp.concatenate([rows_ref[pl.ds(k, 1), :], blank], axis=1)
        spread = pltpu.roll(
            jnp.broadcast_to(tap_row, (pair_rows, lanes)), 0, 1, stride=1, stride_axis=0
        )
        spread = jnp.where(sub < strip_rows, spread, pltpu.roll(spread, pitch - strip_rows, 1))
        row_taps_ref[pl.ds(pl.multiple_of(k * pair_rows, pair_rows), pair_rows), :] = spread
        tap_col = jnp.concatenate([cols_ref[pl.ds(k, 1), :], blank], axis=1)
        band = pltpu.roll(jnp.broadcast_to(tap_col, (lanes, lanes)), 0, 1, stride=1, stride_axis=0)
        for side in range(2):
            kept = jnp.where(keep, band, 0.0) if side == 0 else jnp.where(keep, 0.0, band)
            high, low = split_in_two(kept)
            col_bands_ref[k, 0:lanes, side * lanes : (side + 1) * lanes] = high
            col_bands_ref[k, lanes : 2 * lanes, side * lanes : (side + 1) * lanes] = low
        return carry

    lax.fori_loop(0, bases, one_basis, 0, unroll=bases)
    taps_f32 = row_taps_ref[...]
    taps_f32 = taps_f32 + pltpu.roll(taps_f32, part, 1)
    is_first = lax.rem(iota(taps_f32.shape, 0), pair_rows) < strip_rows
    for c in range(CAP):
        own = jnp.where(is_first, taps_f32, 0.0) if c == 0 else jnp.where(is_first, 0.0, taps_f32)
        for over in range(8):
            high, low = split_in_two(pltpu.roll(own, over, 1) if over else own)
            row_bands_ref[c, over, :, 0:lanes] = high
            row_bands_ref[c, over, :, lanes : 2 * lanes] = low


def fit_group(
    first_pair,
    pairs,
    strip_rows,
    top,
    bases,
    me,
    info_ref,
    stamp_r_ref,
    stamp_c_ref,
    framed_ref,
    pixels_ref,
    row_bands_ref,
    col_bands_ref,
    across_ref,
    design_ref,
    gram_ref,
    out_ref,
):
    lanes = pixels_ref.shape[1]
    pair_rows = CAP * strip_rows
    n_rows = pairs * pair_rows
    stamps = stamp_r_ref.shape[1]
    columns = bases + 1
    padded = up(columns + 1, 8)
    pitch = 2 * lanes // 4 // CAP
    group_rows = pl.ds(pl.multiple_of(first_pair * pair_rows, n_rows), n_rows)

    def filter_rows(p, carry):
        windows = []
        bands = None
        for c in range(CAP):
            at = (first_pair + p) * pair_rows + c * strip_rows
            first = info_ref[pl.ds(at, 1), :][0, 0] + top
            block = info_ref[pl.ds(at + 1, 1), :][0, 0]
            tile = lax.div(first, 8)
            sides = [
                framed_ref[block + side, pl.ds(tile, pitch // 8)].reshape(pitch, lanes)
                for side in range(2)
            ]
            windows.append(jnp.concatenate(sides, axis=1))
            own = row_bands_ref[c, lax.rem(first, 8)]
            bands = own if bands is None else bands + own
        high, low = split_in_two(jnp.concatenate(windows, axis=0))
        stacked = jnp.concatenate([high, low, high, low], axis=0)
        across = jnp.dot(bands, stacked, preferred_element_type=F32)
        across = across[: bases * pair_rows].reshape(bases, pair_rows, 2 * lanes)
        across_ref[:, pl.ds(pl.multiple_of(p * pair_rows, pair_rows), pair_rows), :] = across
        return carry

    lax.fori_loop(0, pairs, filter_rows, 0, unroll=pairs)

    def filter_cols(k, carry):
        high, low = split_in_two(across_ref[k])
        product = contract_last(jnp.concatenate([high, low], axis=0), col_bands_ref[k])
        product = product[:n_rows] + product[n_rows:]
        design_ref[pl.ds(pl.multiple_of(k * n_rows, n_rows), n_rows), :] = (
            product[:, :lanes] + product[:, lanes:]
        )
        return carry

    lax.fori_loop(0, bases, filter_cols, 0, unroll=bases)
    design_ref[bases * n_rows : columns * n_rows, :] = jnp.ones((n_rows, lanes), F32)
    design_ref[columns * n_rows : (columns + 1) * n_rows, :] = pixels_ref[group_rows, :]
    design_ref[(columns + 1) * n_rows :, :] = jnp.zeros(
        ((padded - columns - 1) * n_rows, lanes), F32
    )

    sub = iota((pair_rows, lanes), 0)
    lane = iota((pair_rows, lanes), 1)

    def normal_of(p, carry):
        tile = info_ref[
            pl.ds(pl.multiple_of((first_pair + p) * pair_rows, pair_rows), pair_rows), :
        ]

        def of_pair(item):
            return jnp.where(
                sub < strip_rows, tile[item : item + 1], tile[strip_rows + item : strip_rows + item + 1]
            )

        row_at = (of_pair(0) + lax.rem(sub, strip_rows)).astype(F32)
        col_at = (of_pair(1) * lanes + lane).astype(F32)
        nearest = jnp.full((pair_rows, lanes), 1e9, F32)
        for m in range(stamps):
            row_gap = jnp.abs(row_at - stamp_r_ref[me, m].astype(F32))
            col_gap = jnp.abs(col_at - stamp_c_ref[me, m].astype(F32))
            nearest = jnp.minimum(nearest, jnp.maximum(row_gap, col_gap))
        weight = jnp.where((nearest <= STAMP_HALF) & (of_pair(2) > 0), 1.0, 0.0)
        pieces = []
        for q in range(pair_rows):
            design = design_ref[pl.ds(p * pair_rows + q, padded, stride=n_rows), :]
            pieces.append(design * weight[q : q + 1, :])
        high, low = split_in_two(jnp.concatenate(pieces, axis=1))
        both = jnp.concatenate([high, low], axis=0)
        gram = contract_last(both, both)
        gram_ref[pl.ds(pl.multiple_of(p * padded, padded), padded), 0 : 2 * padded] = (
            gram[:padded] + gram[padded:]
        )
        return carry

    lax.fori_loop(0, pairs, normal_of, 0, unroll=pairs)

    unknown = iota((padded, pairs), 0)
    system = []
    for k in range(columns):
        turned = gram_ref[pl.ds(k, pairs, stride=padded), 0 : 2 * padded].T
        turned = turned[:padded] + turned[padded:]
        system.append(turned + jnp.where(unknown == k, RIDGE, 0.0))
    system = jnp.stack(system)
    for n in range(columns):
        within = n % 8
        if n and within == 0:
            system = system[:, 8:, :]
        pivot = system[n] * (1.0 / system[n, within : within + 1, :])
        rest = system - system[:, within : within + 1, :] * pivot[None]
        parts = [rest[:n], pivot[None], rest[n + 1 :]]
        system = jnp.concatenate([item for item in parts if item.shape[0]], axis=0)
    solved = columns - (columns - 1) // 8 * 8
    coeff = jnp.concatenate(
        [system[k, solved : solved + 1, :] for k in range(columns)]
        + [jnp.zeros((padded - columns, pairs), F32)],
        axis=0,
    ).T
    coeff = jnp.broadcast_to(coeff[:, None, :], (pairs, pair_rows, padded)).reshape(n_rows, padded)
    rest = pixels_ref[group_rows, :]
    for k in range(columns):
        rest = rest - design_ref[k * n_rows : (k + 1) * n_rows, :] * coeff[:, k : k + 1]
    out_ref[group_rows, :] = rest


def exchange(peers, me, pairs_of_refs, per_peer, sends, recvs):
    def rows_of(ref, peer):
        return ref.at[pl.ds(pl.multiple_of(peer * per_peer, per_peer), per_peer), :]

    def copies(offset, there, here):
        return [
            pltpu.make_async_remote_copy(
                src_ref=rows_of(source, there),
                dst_ref=rows_of(target, here),
                send_sem=sends.at[item, offset],
                recv_sem=recvs.at[item, offset],
                device_id={"patch": there},
                device_id_type=MESH,
            )
            for item, (source, target) in enumerate(pairs_of_refs)
        ]

    def start(offset, carry):
        for copy in copies(offset, lax.rem(me + offset, peers), me):
            copy.start()
        return carry

    def finish_recv(offset, carry):
        sender = lax.rem(me + peers - offset, peers)
        for copy in copies(offset, sender, sender):
            copy.wait_recv()
        return carry

    def finish_send(offset, carry):
        for copy in copies(offset, lax.rem(me + offset, peers), me):
            copy.wait_send()
        return carry

    def begin():
        lax.fori_loop(1, peers, start, 0)
        own = pl.ds(pl.multiple_of(me * per_peer, per_peer), per_peer)
        for source, target in pairs_of_refs:
            target[own, :] = source[own, :]

    return (
        begin,
        lambda: lax.fori_loop(1, peers, finish_recv, 0),
        lambda: lax.fori_loop(1, peers, finish_send, 0),
    )


def whole_kernel(
    template_ref,
    science_ref,
    dest_ref,
    offset_ref,
    block_ref,
    rows_ref,
    cols_ref,
    stamp_r_ref,
    stamp_c_ref,
    out_ref,
    row_taps_ref,
    row_bands_ref,
    col_bands_ref,
    across_ref,
    design_ref,
    gram_ref,
    framed_ref,
    left_ref,
    right_ref,
    send_pixels_ref,
    send_info_ref,
    pixels_ref,
    info_ref,
    residual_ref,
    returned_ref,
    go_sends,
    go_recvs,
    back_sends,
    back_recvs,
    halo_sends,
    halo_recvs,
):
    peers = lax.axis_size("patch")
    me = lax.axis_index("patch")
    strips, strip_rows, lanes = science_ref.shape
    sub_rows, sub_cols = template_ref.shape
    bases, taps = rows_ref.shape
    half = (taps - 1) // 2
    slots = peers * CAP
    pair_rows = CAP * strip_rows
    pairs = math.gcd(peers, 16)

    barrier = pltpu.get_barrier_semaphore()

    def greet(offset, carry):
        pl.semaphore_signal(
            barrier,
            inc=1,
            device_id={"patch": lax.rem(me + offset, peers)},
            device_id_type=MESH,
        )
        return carry

    lax.fori_loop(1, peers, greet, 0)

    strip_goes, slot_holds = routes_of(dest_ref, peers)
    strip_hot = jnp.where(strip_goes, 1.0, 0.0)
    slot_hot = jnp.where(slot_holds, 1.0, 0.0)
    for r in range(strip_rows):
        send_pixels_ref[pl.ds(r, slots, stride=strip_rows), :] = exact_dot(
            slot_hot, science_ref[:, r, :]
        )
    one = jnp.ones(offset_ref.shape, jnp.int32)
    for item, values in enumerate((offset_ref[...], block_ref[...], one)):
        chosen = jnp.sum(jnp.where(slot_holds, values, 0), axis=1, keepdims=True)
        send_info_ref[pl.ds(item, slots, stride=strip_rows), :] = jnp.broadcast_to(
            chosen, (slots, lanes)
        )
    send_info_ref[pl.ds(3, slots, stride=strip_rows), :] = jnp.zeros((slots, lanes), jnp.int32)

    go, go_recv, go_send = exchange(
        peers,
        me,
        ((send_info_ref, info_ref), (send_pixels_ref, pixels_ref)),
        pair_rows,
        go_sends,
        go_recvs,
    )
    back, back_recv, back_send = exchange(
        peers, me, ((residual_ref, returned_ref),), pair_rows, back_sends, back_recvs
    )
    halos = [
        pltpu.make_async_remote_copy(
            src_ref=template_ref.at[:, pl.ds(source, lanes)],
            dst_ref=target,
            send_sem=halo_sends.at[side],
            recv_sem=halo_recvs.at[side],
            device_id={"patch": lax.rem(me + move, peers)},
            device_id_type=MESH,
        )
        for side, (source, target, move) in enumerate(
            ((sub_cols - lanes, left_ref, 1), (0, right_ref, peers - 1))
        )
    ]

    pl.semaphore_wait(barrier, peers - 1)
    for copy in halos:
        copy.start()
    go()

    build_bands(rows_ref, cols_ref, row_taps_ref, row_bands_ref, col_bands_ref, strip_rows)
    top = up(half, 8)
    blocks, tiles = framed_ref.shape[:2]
    above, below = top // 8, (top + sub_rows) // 8
    framed_ref[:, 0:above] = jnp.zeros((blocks, above, 8, lanes), F32)
    framed_ref[:, below:] = jnp.zeros((blocks, tiles - below, 8, lanes), F32)
    for copy in halos:
        copy.wait_recv()
    left = jnp.where(me > 0, left_ref[...], 0.0)
    right = jnp.where(me < peers - 1, right_ref[...], 0.0)
    lane = iota((sub_rows, lanes), 1)
    wide = jnp.concatenate([template_ref[...], jnp.where(lane < half, right, 0.0)], axis=1)
    wide = pltpu.roll(wide, half, 1)
    first_block = jnp.where(lane < half, pltpu.roll(left, half, 1), wide[:, :lanes])
    for b in range(blocks):
        own = first_block if b == 0 else wide[:, b * lanes : (b + 1) * lanes]
        framed_ref[b, above:below] = own.reshape(below - above, 8, lanes)
    go_recv()

    def one_group(group):
        fit_group(
            group * pairs,
            pairs,
            strip_rows,
            top - half,
            bases,
            me,
            info_ref,
            stamp_r_ref,
            stamp_c_ref,
            framed_ref,
            pixels_ref,
            row_bands_ref,
            col_bands_ref,
            across_ref,
            design_ref,
            gram_ref,
            residual_ref,
        )

    if peers == pairs:
        one_group(0)
    else:
        pl.loop(0, peers // pairs)(one_group)

    back()
    back_recv()
    for r in range(strip_rows):
        out_ref[:, r, :] = exact_dot(
            strip_hot, returned_ref[pl.ds(r, slots, stride=strip_rows), :]
        )
    for copy in halos:
        copy.wait_send()
    go_send()
    back_send()


def on_device(
    template, science, dest, row_offset, col_block, basis_rows, basis_cols, stamp_rows, stamp_cols
):
    peers = lax.axis_size("patch")
    strips, strip_rows, lanes = science.shape
    sub_rows, sub_cols = template.shape
    bases, taps = basis_rows.shape
    pair_rows = CAP * strip_rows
    pairs = math.gcd(peers, 16)
    n_rows = pairs * pair_rows
    padded = up(bases + 2, 8)
    even = up(bases, 2)
    pitch = 2 * lanes // 4 // CAP
    half = (taps - 1) // 2
    tiles = (sub_rows - strip_rows + up(half, 8) - half) // 8 + pitch // 8
    smem = pl.BlockSpec(memory_space=pltpu.SMEM)
    vmem = pl.BlockSpec(memory_space=pltpu.VMEM)
    sems = pltpu.SemaphoreType.DMA
    return pl.pallas_call(
        whole_kernel,
        out_shape=jax.ShapeDtypeStruct(science.shape, F32),
        in_specs=[vmem] * 7 + [smem] * 2,
        out_specs=vmem,
        scratch_shapes=[
            pltpu.VMEM((even * pair_rows, lanes), F32),
            pltpu.VMEM((CAP, 8, even * pair_rows, 2 * lanes), BF16),
            pltpu.VMEM((bases, 2 * lanes, 2 * lanes), BF16),
            pltpu.VMEM((bases, n_rows, 2 * lanes), F32),
            pltpu.VMEM((padded * n_rows, lanes), F32),
            pltpu.VMEM((pairs * padded, lanes), F32),
            pltpu.VMEM((sub_cols // lanes + 1, tiles, 8, lanes), F32),
            pltpu.VMEM((sub_rows, lanes), F32),
            pltpu.VMEM((sub_rows, lanes), F32),
            pltpu.VMEM((peers * pair_rows, lanes), F32),
            pltpu.VMEM((peers * pair_rows, lanes), jnp.int32),
            pltpu.VMEM((peers * pair_rows, lanes), F32),
            pltpu.VMEM((peers * pair_rows, lanes), jnp.int32),
            pltpu.VMEM((peers * pair_rows, lanes), F32),
            pltpu.VMEM((peers * pair_rows, lanes), F32),
            sems((2, peers)),
            sems((2, peers)),
            sems((1, peers)),
            sems((1, peers)),
            sems((2,)),
            sems((2,)),
        ],
        compiler_params=pltpu.CompilerParams(
            collective_id=0, has_side_effects=True, vmem_limit_bytes=48 << 20
        ),
    )(
        template,
        science,
        dest,
        row_offset.reshape(1, strips),
        col_block.reshape(1, strips),
        basis_rows,
        basis_cols,
        stamp_rows,
        stamp_cols,
    )


def solution(mesh):
    placed = (
        P(None, ("groups", "patch")),
        P(("groups", "patch"), None, None),
        P(("groups", "patch"), None),
        P(("groups", "patch")),
        P(("groups", "patch")),
        P(),
        P(),
        P("groups", None),
        P("groups", None),
    )
    return jax.shard_map(
        on_device,
        mesh=mesh,
        in_specs=placed,
        out_specs=P(("groups", "patch"), None, None),
        check_vma=False,
    )
```

time: 341 us -> 26.7 us (0.08)
  other arithmetic: 171 us -> 0 us
  local copies, waits for them, and re-layouts: 126 us -> 3.27 us
  starting transfers between devices: 24.5 us -> 0 us
  Pallas kernels: 0 us -> 23.1 us
  matrix products: 9.49 us -> 0 us
  waiting for transfers between devices: 7.36 us -> 0 us
    gather x96 -> x0, local copies, waits for them, and re-layouts: 113 us -> none
    add x6 -> x0, other arithmetic: 93.8 us -> none  [the longest x1 73.2 us: filter_field(): result + row_taps[shift_tap] * across[shift_tap:shift_tap + out_rows, :]]
    another operation x7 -> x0, other arithmetic: 76 us -> none  [the longest x4 41.2 us: factor_of(): return jnp.linalg.cholesky(pair_normal)]
    pallas_call x0 -> x1, Pallas kernels: none -> 23.1 us  [on_device(): pl.pallas_call(whole_kernel, out_shape=jax.ShapeDtypeStruct(science.shape...]
    all_to_all x3 -> x0, starting transfers between devices: 20.8 us -> none  [the longest x1 9.3 us: on_device(): lax.all_to_all(slot_info, 'patch', split_axis=0, concat_axis=0, tiled=True)]
    all_to_all x3 -> x0, waiting for transfers between devices: 7.36 us -> none  [the longest x1 6.87 us: on_device(): lax.all_to_all(residuals, 'patch', split_axis=0, concat_axis=0, tiled=True)]
    dot_general x6 -> x0, matrix products: 7.08 us -> none  [the longest x1 2.11 us: factor_of(): normal = jnp.einsum('skp,slp->skl', weighted, design, precision=HIGH)]
    ppermute x2 -> x0, starting transfers between devices: 3.64 us -> none  [the longest x1 2.35 us: with_halo(): lax.ppermute(tail, axis, [(i, (i + 1) % count) for i in range(ends)])]
  transfers between devices with their start and end apart: 5 -> 0, of which waited for: 2 -> 0; matrix products, arithmetic and copies ran while one was open for 89% -> 0% of each run, Pallas kernels for 0% -> 0%
where the time goes in v2:
time: 26.7 us; the launch traced here: 26.4 us
  Pallas kernels  23.1 us (87%)
  local copies, waits for them, and re-layouts  3.27 us (12%)
    pallas_call x1, Pallas kernels, on_device(): pl.pallas_call(whole_kernel, out_shape=jax.ShapeDtypeStruct(science.shape...  23.1 us
    unnamed x18, local copies, waits for them, and re-layouts  3.27 us

profile of v2, /device:TPU:0, one launch (start us, length us, event | category | flops | bytes accessed | tf_op | source)
XLA Modules:
  0.0 26.4 jit_solution(10699780832985267137)
XLA Ops:
  0.0 0.0 copy-start.6
  0.0 0.0 copy-start.1
  0.0 0.7 %copy.10.dest_ref = s32[16,1]{1,0:T(8,128)S(1)} copy(s32[16,1]{0,1:T(1,128)} %param.11) | data formatting | bytes 128 | tf_op args[2]
  0.8 0.0 copy-done.6
  0.8 0.1 copy.11.rows_ref
  0.8 0.0 copy-start.2
  0.9 0.0 copy-start.3
  0.9 0.0 copy-start.4
  0.9 0.0 copy-start.5
  0.9 0.8 %copy.12.cols_ref = f32[27,21]{1,0:T(8,128)S(1)} copy(f32[27,21]{0,1:T(8,128)} %param.15) | data formatting | bytes 4536 | tf_op args[6]
  1.7 0.0 copy-done.1
  1.7 0.0 copy-done.2
  1.7 0.0 copy-done.3
  1.7 0.0 copy-done.4
  1.7 0.0 copy-done.5
  1.7 0.0 copy-start
  1.7 0.9 %copy-done = f32[64,1024]{1,0:T(8,128)S(1)} copy-done((f32[64,1024]{1,0:T(8,128)S(1)}, f32[64,1024]{1,0:T(8,128)}, u32[]{:S(2)}) %copy-start) | copy-done | bytes 262168
  2.7 23.1 %shard_map.91 = f32[16,4,128]{2,1,0:T(4,128)S(1)} custom-call(f32[64,1024]{1,0:T(8,128)S(1)} %copy-done, f32[16,4,128]{2,1,0:T(4,128)S(1)} %copy-done.1, s32[16,1]{1,0:T(8,128)S(1)} %copy.10.dest_ref, s32[1,16]{1,0:T(1,128)S(1)} %bitcast.2, s32[1,16]{1,0:T(1,128)S(1)} %bitcast.3, f32[27,21]{1,0:T(8,128)S(1)} %copy.11.rows_ref, f32[27,21]{1,0:T(8,128)S(1)} %copy.12.cols_ref, ...), custom_call_target="tpu_custom_call" | custom-call | tf_op jit(solution)/shard_map/pallas_call | solution.py:447
  25.8 0.6 %copy.14 = f32[16,4,128]{2,1,0:T(4,128)} copy(f32[16,4,128]{2,1,0:T(4,128)S(1)} %shard_map.91) | data formatting | bytes 65536
Async XLA Ops:
  0.0 0.8 %copy-start.6 = (f32[27,21]{0,1:T(8,128)S(1)}, f32[27,21]{0,1:T(8,128)}, u32[]{:S(2)}) copy-start(f32[27,21]{0,1:T(8,128)} %param.14) | copy-start | bytes 6808
  0.0 1.7 %copy-start.1 = (f32[16,4,128]{2,1,0:T(4,128)S(1)}, f32[16,4,128]{2,1,0:T(4,128)}, u32[]{:S(2)}) copy-start(f32[16,4,128]{2,1,0:T(4,128)} %science_ref.1) | copy-start | bytes 98308
  0.8 0.9 %copy-start.2 = (s32[16,24]{1,0:T(8,128)S(1)}, s32[16,24]{1,0:T(8,128)}, u32[]{:S(2)}) copy-start(s32[16,24]{1,0:T(8,128)} %stamp_r_ref.1) | copy-start | bytes 4612
  0.9 0.9 %copy-start.3 = (s32[16,24]{1,0:T(8,128)S(1)}, s32[16,24]{1,0:T(8,128)}, u32[]{:S(2)}) copy-start(s32[16,24]{1,0:T(8,128)} %stamp_c_ref.1) | copy-start | bytes 4612
  0.9 0.9 %copy-start.4 = (s32[16]{0:T(128)S(1)}, s32[16]{0:T(128)}, u32[]{:S(2)}) copy-start(s32[16]{0:T(128)} %param.12) | copy-start | bytes 196
  0.9 0.9 %copy-start.5 = (s32[16]{0:T(128)S(1)}, s32[16]{0:T(128)}, u32[]{:S(2)}) copy-start(s32[16]{0:T(128)} %param.13) | copy-start | bytes 196
  1.7 1.0 %copy-start = (f32[64,1024]{1,0:T(8,128)S(1)}, f32[64,1024]{1,0:T(8,128)}, u32[]{:S(2)}) copy-start(f32[64,1024]{1,0:T(8,128)} %template_ref.1) | copy-start | bytes 786436

commit v3 on v2

--- a/solution.py
+++ b/solution.py
@@ -12,6 +12,8 @@
 RIDGE = 1.0
 HIGH = lax.Precision.HIGHEST
 MESH = pl.DeviceIdType.MESH
+ITEMS = 3
+NOWHERE = -(1 << 20)
 F32 = jnp.float32
 BF16 = jnp.bfloat16
 
@@ -37,23 +39,20 @@
     return lax.broadcasted_iota(jnp.int32, shape, dim)
 
 
-def routes_of(dest_ref, peers):
-    strips = dest_ref.shape[0]
-    slots = peers * CAP
+def routes_of(targets, peers):
+    strips = targets.shape[1]
     square = (strips, strips)
     down, across = iota(square, 0), iota(square, 1)
-    target_down = jnp.broadcast_to(dest_ref[...], square)
-    target_across = jnp.sum(jnp.where(down == across, target_down, 0), axis=0, keepdims=True)
+    target_across = jnp.broadcast_to(targets, square)
+    target_down = jnp.sum(jnp.where(down == across, target_across, 0), axis=1, keepdims=True)
     same = jnp.where(target_down == target_across, 1, 0)
     rank_down = jnp.sum(jnp.where(across < down, same, 0), axis=1, keepdims=True)
     rank_across = jnp.sum(jnp.where(down < across, same, 0), axis=0, keepdims=True)
-    slot_down = target_down[:, 0:1] * CAP + rank_down
-    slot_across = target_across * CAP + rank_across
-    return slot_down == iota((strips, slots), 1), slot_across == iota((slots, strips), 0)
-
-
-def build_bands(rows_ref, cols_ref, row_taps_ref, row_bands_ref, col_bands_ref, strip_rows):
-    bases, taps = rows_ref.shape
+    return target_down * CAP + rank_down, targets * CAP + rank_across
+
+
+def build_bands(row_basis, col_basis, row_taps_ref, row_bands_ref, col_bands_ref, strip_rows):
+    bases, taps = row_basis.shape
     lanes = row_taps_ref.shape[1]
     pair_rows = CAP * strip_rows
     part = 2 * lanes // 4
@@ -63,23 +62,20 @@
     row_taps_ref[...] = jnp.zeros_like(row_taps_ref)
     blank = jnp.zeros((1, lanes - taps), F32)
 
-    def one_basis(k, carry):
-        tap_row = jnp.concatenate([rows_ref[pl.ds(k, 1), :], blank], axis=1)
+    for k in range(bases):
+        tap_row = jnp.concatenate([row_basis[k : k + 1, :], blank], axis=1)
         spread = pltpu.roll(
             jnp.broadcast_to(tap_row, (pair_rows, lanes)), 0, 1, stride=1, stride_axis=0
         )
         spread = jnp.where(sub < strip_rows, spread, pltpu.roll(spread, pitch - strip_rows, 1))
-        row_taps_ref[pl.ds(pl.multiple_of(k * pair_rows, pair_rows), pair_rows), :] = spread
-        tap_col = jnp.concatenate([cols_ref[pl.ds(k, 1), :], blank], axis=1)
+        row_taps_ref[k * pair_rows : (k + 1) * pair_rows, :] = spread
+        tap_col = jnp.concatenate([col_basis[k : k + 1, :], blank], axis=1)
         band = pltpu.roll(jnp.broadcast_to(tap_col, (lanes, lanes)), 0, 1, stride=1, stride_axis=0)
         for side in range(2):
             kept = jnp.where(keep, band, 0.0) if side == 0 else jnp.where(keep, 0.0, band)
             high, low = split_in_two(kept)
             col_bands_ref[k, 0:lanes, side * lanes : (side + 1) * lanes] = high
             col_bands_ref[k, lanes : 2 * lanes, side * lanes : (side + 1) * lanes] = low
-        return carry
-
-    lax.fori_loop(0, bases, one_basis, 0, unroll=bases)
     taps_f32 = row_taps_ref[...]
     taps_f32 = taps_f32 + pltpu.roll(taps_f32, part, 1)
     is_first = lax.rem(iota(taps_f32.shape, 0), pair_rows) < strip_rows
@@ -109,6 +105,7 @@
     design_ref,
     gram_ref,
     out_ref,
+    await_pixels,
 ):
     lanes = pixels_ref.shape[1]
     pair_rows = CAP * strip_rows
@@ -123,9 +120,9 @@
         windows = []
         bands = None
         for c in range(CAP):
-            at = (first_pair + p) * pair_rows + c * strip_rows
-            first = info_ref[pl.ds(at, 1), :][0, 0] + top
-            block = info_ref[pl.ds(at + 1, 1), :][0, 0]
+            info = info_ref[first_pair + p]
+            first = info[0, ITEMS * c] + top
+            block = info[0, ITEMS * c + 1]
             tile = lax.div(first, 8)
             sides = [
                 framed_ref[block + side, pl.ds(tile, pitch // 8)].reshape(pitch, lanes)
@@ -153,6 +150,7 @@
         return carry
 
     lax.fori_loop(0, bases, filter_cols, 0, unroll=bases)
+    await_pixels()
     design_ref[bases * n_rows : columns * n_rows, :] = jnp.ones((n_rows, lanes), F32)
     design_ref[columns * n_rows : (columns + 1) * n_rows, :] = pixels_ref[group_rows, :]
     design_ref[(columns + 1) * n_rows :, :] = jnp.zeros(
@@ -163,23 +161,19 @@
     lane = iota((pair_rows, lanes), 1)
 
     def normal_of(p, carry):
-        tile = info_ref[
-            pl.ds(pl.multiple_of((first_pair + p) * pair_rows, pair_rows), pair_rows), :
-        ]
+        info = info_ref[first_pair + p]
 
         def of_pair(item):
-            return jnp.where(
-                sub < strip_rows, tile[item : item + 1], tile[strip_rows + item : strip_rows + item + 1]
-            )
-
-        row_at = (of_pair(0) + lax.rem(sub, strip_rows)).astype(F32)
+            return jnp.where(sub < strip_rows, info[0, item], info[0, ITEMS + item])
+
+        row_at = (of_pair(2) + lax.rem(sub, strip_rows)).astype(F32)
         col_at = (of_pair(1) * lanes + lane).astype(F32)
         nearest = jnp.full((pair_rows, lanes), 1e9, F32)
         for m in range(stamps):
             row_gap = jnp.abs(row_at - stamp_r_ref[me, m].astype(F32))
             col_gap = jnp.abs(col_at - stamp_c_ref[me, m].astype(F32))
             nearest = jnp.minimum(nearest, jnp.maximum(row_gap, col_gap))
-        weight = jnp.where((nearest <= STAMP_HALF) & (of_pair(2) > 0), 1.0, 0.0)
+        weight = jnp.where(nearest <= STAMP_HALF, 1.0, 0.0)
         pieces = []
         for q in range(pair_rows):
             design = design_ref[pl.ds(p * pair_rows + q, padded, stride=n_rows), :]
@@ -224,6 +218,8 @@
 
 def exchange(peers, me, pairs_of_refs, per_peer, sends, recvs):
     def rows_of(ref, peer):
+        if len(ref.shape) == 3:
+            return ref.at[peer]
         return ref.at[pl.ds(pl.multiple_of(peer * per_peer, per_peer), per_peer), :]
 
     def copies(offset, there, here):
@@ -259,7 +255,10 @@
         lax.fori_loop(1, peers, start, 0)
         own = pl.ds(pl.multiple_of(me * per_peer, per_peer), per_peer)
         for source, target in pairs_of_refs:
-            target[own, :] = source[own, :]
+            if len(source.shape) == 3:
+                target[me] = source[me]
+            else:
+                target[own, :] = source[own, :]
 
     return (
         begin,
@@ -269,6 +268,16 @@
 
 
 def whole_kernel(
+    template_hbm,
+    science_hbm,
+    dest_hbm,
+    offset_hbm,
+    block_hbm,
+    rows_hbm,
+    cols_hbm,
+    stamp_r_hbm,
+    stamp_c_hbm,
+    out_ref,
     template_ref,
     science_ref,
     dest_ref,
@@ -278,7 +287,6 @@
     cols_ref,
     stamp_r_ref,
     stamp_c_ref,
-    out_ref,
     row_taps_ref,
     row_bands_ref,
     col_bands_ref,
@@ -294,18 +302,21 @@
     info_ref,
     residual_ref,
     returned_ref,
+    info_sends,
+    info_recvs,
     go_sends,
     go_recvs,
     back_sends,
     back_recvs,
     halo_sends,
     halo_recvs,
+    fetched,
 ):
     peers = lax.axis_size("patch")
     me = lax.axis_index("patch")
     strips, strip_rows, lanes = science_ref.shape
     sub_rows, sub_cols = template_ref.shape
-    bases, taps = rows_ref.shape
+    taps, bases = rows_ref.shape
     half = (taps - 1) // 2
     slots = peers * CAP
     pair_rows = CAP * strip_rows
@@ -323,29 +334,50 @@
         return carry
 
     lax.fori_loop(1, peers, greet, 0)
-
-    strip_goes, slot_holds = routes_of(dest_ref, peers)
-    strip_hot = jnp.where(strip_goes, 1.0, 0.0)
-    slot_hot = jnp.where(slot_holds, 1.0, 0.0)
-    for r in range(strip_rows):
-        send_pixels_ref[pl.ds(r, slots, stride=strip_rows), :] = exact_dot(
-            slot_hot, science_ref[:, r, :]
-        )
-    one = jnp.ones(offset_ref.shape, jnp.int32)
-    for item, values in enumerate((offset_ref[...], block_ref[...], one)):
-        chosen = jnp.sum(jnp.where(slot_holds, values, 0), axis=1, keepdims=True)
-        send_info_ref[pl.ds(item, slots, stride=strip_rows), :] = jnp.broadcast_to(
-            chosen, (slots, lanes)
-        )
-    send_info_ref[pl.ds(3, slots, stride=strip_rows), :] = jnp.zeros((slots, lanes), jnp.int32)
-
+    fetches = [
+        pltpu.make_async_copy(source, target, fetched.at[item])
+        for item, (source, target) in enumerate(
+            (
+                (dest_hbm, dest_ref),
+                (offset_hbm, offset_ref),
+                (block_hbm, block_ref),
+                (science_hbm, science_ref),
+                (template_hbm, template_ref),
+                (rows_hbm, rows_ref),
+                (cols_hbm, cols_ref),
+                (stamp_r_hbm, stamp_r_ref),
+                (stamp_c_hbm, stamp_c_ref),
+            )
+        )
+    ]
+    for fetch in fetches:
+        fetch.start()
+    top = up(half, 8)
+    blocks, tiles = framed_ref.shape[:2]
+    above, below = top // 8, (top + sub_rows) // 8
+    framed_ref[:, 0:above] = jnp.zeros((blocks, above, 8, lanes), F32)
+    framed_ref[:, below:] = jnp.zeros((blocks, tiles - below, 8, lanes), F32)
+    for fetch in fetches[:4]:
+        fetch.wait()
+
+    slot_down, slot_across = routes_of(dest_ref[...], peers)
+    info_lane = iota((peers, lanes), 1)
+    info = jnp.zeros((peers, lanes), jnp.int32)
+    for c in range(CAP):
+        holds = slot_across == iota((peers, strips), 0) * CAP + c
+        for item, (values, empty) in enumerate(
+            ((offset_ref[...], 0), (block_ref[...], 0), (offset_ref[...], NOWHERE))
+        ):
+            chosen = empty + jnp.sum(
+                jnp.where(holds, values - empty, 0), axis=1, keepdims=True
+            )
+            info = jnp.where(info_lane == ITEMS * c + item, chosen, info)
+    send_info_ref[:, 0, :] = info
+    tell, tell_recv, tell_send = exchange(
+        peers, me, ((send_info_ref, info_ref),), pair_rows, info_sends, info_recvs
+    )
     go, go_recv, go_send = exchange(
-        peers,
-        me,
-        ((send_info_ref, info_ref), (send_pixels_ref, pixels_ref)),
-        pair_rows,
-        go_sends,
-        go_recvs,
+        peers, me, ((send_pixels_ref, pixels_ref),), pair_rows, go_sends, go_recvs
     )
     back, back_recv, back_send = exchange(
         peers, me, ((residual_ref, returned_ref),), pair_rows, back_sends, back_recvs
@@ -364,19 +396,38 @@
         )
     ]
 
+    slot_hot = jnp.where(slot_across == iota((slots, strips), 0), 1.0, 0.0)
+    for r in range(strip_rows):
+        send_pixels_ref[pl.ds(r, slots, stride=strip_rows), :] = exact_dot(
+            slot_hot, science_ref[:, r, :]
+        )
+    fetches[4].wait()
     pl.semaphore_wait(barrier, peers - 1)
-    for copy in halos:
-        copy.start()
+    tell()
+
+    @pl.when(me < peers - 1)
+    def _():
+        halos[0].start()
+
+    @pl.when(me > 0)
+    def _():
+        halos[1].start()
+
     go()
 
-    build_bands(rows_ref, cols_ref, row_taps_ref, row_bands_ref, col_bands_ref, strip_rows)
-    top = up(half, 8)
-    blocks, tiles = framed_ref.shape[:2]
-    above, below = top // 8, (top + sub_rows) // 8
-    framed_ref[:, 0:above] = jnp.zeros((blocks, above, 8, lanes), F32)
-    framed_ref[:, below:] = jnp.zeros((blocks, tiles - below, 8, lanes), F32)
-    for copy in halos:
-        copy.wait_recv()
+    for fetch in fetches[5:]:
+        fetch.wait()
+    build_bands(
+        rows_ref[...].T, cols_ref[...].T, row_taps_ref, row_bands_ref, col_bands_ref, strip_rows
+    )
+    @pl.when(me > 0)
+    def _():
+        halos[0].wait_recv()
+
+    @pl.when(me < peers - 1)
+    def _():
+        halos[1].wait_recv()
+
     left = jnp.where(me > 0, left_ref[...], 0.0)
     right = jnp.where(me < peers - 1, right_ref[...], 0.0)
     lane = iota((sub_rows, lanes), 1)
@@ -386,7 +437,9 @@
     for b in range(blocks):
         own = first_block if b == 0 else wide[:, b * lanes : (b + 1) * lanes]
         framed_ref[b, above:below] = own.reshape(below - above, 8, lanes)
-    go_recv()
+    tell_recv()
+    if peers != pairs:
+        go_recv()
 
     def one_group(group):
         fit_group(
@@ -407,6 +460,7 @@
             design_ref,
             gram_ref,
             residual_ref,
+            go_recv if peers == pairs else lambda: None,
         )
 
     if peers == pairs:
@@ -416,12 +470,21 @@
 
     back()
     back_recv()
+    strip_hot = jnp.where(slot_down == iota((strips, slots), 1), 1.0, 0.0)
     for r in range(strip_rows):
         out_ref[:, r, :] = exact_dot(
             strip_hot, returned_ref[pl.ds(r, slots, stride=strip_rows), :]
         )
-    for copy in halos:
-        copy.wait_send()
+
+    @pl.when(me < peers - 1)
+    def _():
+        halos[0].wait_send()
+
+    @pl.when(me > 0)
+    def _():
+        halos[1].wait_send()
+
+    tell_send()
     go_send()
     back_send()
 
@@ -441,15 +504,23 @@
     pitch = 2 * lanes // 4 // CAP
     half = (taps - 1) // 2
     tiles = (sub_rows - strip_rows + up(half, 8) - half) // 8 + pitch // 8
-    smem = pl.BlockSpec(memory_space=pltpu.SMEM)
     vmem = pl.BlockSpec(memory_space=pltpu.VMEM)
     sems = pltpu.SemaphoreType.DMA
     return pl.pallas_call(
         whole_kernel,
         out_shape=jax.ShapeDtypeStruct(science.shape, F32),
-        in_specs=[vmem] * 7 + [smem] * 2,
+        in_specs=[pl.BlockSpec(memory_space=pltpu.HBM)] * 9,
         out_specs=vmem,
         scratch_shapes=[
+            pltpu.VMEM(template.shape, F32),
+            pltpu.VMEM(science.shape, F32),
+            pltpu.VMEM((1, strips), jnp.int32),
+            pltpu.VMEM((1, strips), jnp.int32),
+            pltpu.VMEM((1, strips), jnp.int32),
+            pltpu.VMEM((taps, bases), F32),
+            pltpu.VMEM((taps, bases), F32),
+            pltpu.SMEM(stamp_rows.shape, jnp.int32),
+            pltpu.SMEM(stamp_cols.shape, jnp.int32),
             pltpu.VMEM((even * pair_rows, lanes), F32),
             pltpu.VMEM((CAP, 8, even * pair_rows, 2 * lanes), BF16),
             pltpu.VMEM((bases, 2 * lanes, 2 * lanes), BF16),
@@ -460,29 +531,32 @@
             pltpu.VMEM((sub_rows, lanes), F32),
             pltpu.VMEM((sub_rows, lanes), F32),
             pltpu.VMEM((peers * pair_rows, lanes), F32),
-            pltpu.VMEM((peers * pair_rows, lanes), jnp.int32),
+            pltpu.VMEM((peers, 1, lanes), jnp.int32),
             pltpu.VMEM((peers * pair_rows, lanes), F32),
-            pltpu.VMEM((peers * pair_rows, lanes), jnp.int32),
+            pltpu.VMEM((peers, 1, lanes), jnp.int32),
             pltpu.VMEM((peers * pair_rows, lanes), F32),
             pltpu.VMEM((peers * pair_rows, lanes), F32),
-            sems((2, peers)),
-            sems((2, peers)),
+            sems((1, peers)),
+            sems((1, peers)),
+            sems((1, peers)),
+            sems((1, peers)),
             sems((1, peers)),
             sems((1, peers)),
             sems((2,)),
             sems((2,)),
+            sems((9,)),
         ],
         compiler_params=pltpu.CompilerParams(
-            collective_id=0, has_side_effects=True, vmem_limit_bytes=48 << 20
+            collective_id=0, has_side_effects=True, vmem_limit_bytes=62 << 20
         ),
     )(
         template,
         science,
-        dest,
+        dest.reshape(1, strips),
         row_offset.reshape(1, strips),
         col_block.reshape(1, strips),
-        basis_rows,
-        basis_cols,
+        basis_rows.T,
+        basis_cols.T,
         stamp_rows,
         stamp_cols,
     )

time: 26.7 us -> 22.9 us (0.86)
  local copies, waits for them, and re-layouts: 3.27 us -> 1.38 us
  Pallas kernels: 23.1 us -> 21.4 us
    unnamed x18 -> x1, local copies, waits for them, and re-layouts: 3.27 us -> 1.38 us
    pallas_call x1, Pallas kernels: 23.1 us -> 21.4 us  [on_device(): pl.pallas_call(whole_kernel, out_shape=jax.ShapeDtypeStruct(science.shape...]
where the time goes in v3:
time: 22.9 us; the launch traced here: 22.8 us
  Pallas kernels  21.4 us (93%)
  local copies, waits for them, and re-layouts  1.38 us (6%)
    pallas_call x1, Pallas kernels, on_device(): pl.pallas_call(whole_kernel, out_shape=jax.ShapeDtypeStruct(science.shape...  21.4 us
    unnamed x1, local copies, waits for them, and re-layouts  1.38 us

profile of v3, /device:TPU:0, one launch (start us, length us, event | category | flops | bytes accessed | tf_op | source)
XLA Modules:
  0.0 22.8 jit_solution(8118573812848818758)
XLA Ops:
  0.0 21.4 %shard_map.91 = f32[16,4,128]{2,1,0:T(4,128)} custom-call(f32[64,1024]{1,0:T(8,128)} %template_hbm.1, f32[16,4,128]{2,1,0:T(4,128)} %science_hbm.1, s32[1,16]{1,0:T(1,128)} %bitcast.7, s32[1,16]{1,0:T(1,128)} %bitcast.8, s32[1,16]{1,0:T(1,128)} %bitcast.9, f32[21,27]{1,0:T(8,128)} %bitcast.5, f32[21,27]{1,0:T(8,128)} %bitcast.6, s32[16,24]{1,0:T(8,128)} %stamp_r_hbm.1, ...), custom_call_target="tpu_custom_call" | custom-call | tf_op jit(solution)/shard_map/pallas_call | solution.py:509
  21.4 1.4 %copy.11 = f32[16,4,128]{2,1,0:T(4,128)} copy(f32[16,4,128]{2,1,0:T(4,128)} %shard_map.91) | data formatting | bytes 65536
